TPU v7x, 512 devices: a whole 4x8x8 slice. The times are simulated.
512 devices in a mesh: row: 16 (over z, y_lo), col: 32 (over y_hi, x, core).
Axes of the slice: x: 4, y: 8 (y_hi: 4, y_lo: 2; y = y_hi * 2 + y_lo), z: 8, core: 2. Of those that a mesh axis runs over, the one named last changes fastest.
Arguments:
- x_feat: bfloat16 [65536, 256], P('col', 'row'), may hold values from -6 to 6
- weight: bfloat16 [256, 256], replicated, may hold values from -0.375 to 0.375
- tile_vals: bfloat16 [16, 32, 96, 128, 128], P('row', 'col'), may hold values from -0.0546875 to 0.0546875
- tile_row: int32 [16, 32, 96], P('row', 'col'), may hold values from 0 to 31
- tile_col: int32 [16, 32, 96], P('row', 'col'), may hold values from 0 to 15
- tile_live: int32 [16, 32, 96], P('row', 'col'), may hold values from 0 to 1, as said below
- d_out: bfloat16 [65536, 256], P(('row', 'col')), may hold values from -6 to 6
Outputs:
- layer_out: bfloat16 [65536, 256], P(('row', 'col'))
- weight_grad: float32 [256, 256], replicated
- feat_grad: bfloat16 [65536, 256], P('col', 'row')
Inputs may be any that keep to these rules, and one draw needn't show every extreme that they name: `tile_live`: every device has at least max(24, 1) live slots, and in every draw some device has all 96 live.
All inputs are finite; a program needn't handle non-finite values.
Results may differ from a plain program's by a relative error of at most 0.024.
Values may be sent and summed in bfloat16 or wider, within the bound.
A program may use at most 64 MiB of HBM per device.

v0:
```python
import math

import jax
import jax.numpy as jnp
from jax import lax
from jax.sharding import PartitionSpec as P

TILE = 128


def slot_products(vals, index, feats, transpose):
    width = feats.shape[1]
    ftiles = feats.reshape(-1, TILE, width)
    picked = jnp.take(ftiles, index, axis=0)
    if transpose:
        return jnp.einsum("sji,sjf->sif", vals, picked, preferred_element_type=jnp.float32)
    return jnp.einsum("sij,sjf->sif", vals, picked, preferred_element_type=jnp.float32)


def place_tiles(prods, target, live, count_tiles):
    outputs = jnp.arange(count_tiles, dtype=jnp.int32)
    onehot = ((target[None, :] == outputs[:, None]) & (live[None, :] > 0)).astype(jnp.float32)
    placed = jnp.einsum("ts,sif->tif", onehot, prods)
    return placed.reshape(count_tiles * TILE, prods.shape[2])


def local(x_feat, weight, tile_vals, tile_row, tile_col, tile_live, d_out):
    n_row = lax.axis_size("row")
    n_col = lax.axis_size("col")
    own_rows = d_out.shape[0]
    block_rows = own_rows * n_col
    col_nodes = x_feat.shape[0]
    vals = tile_vals[0, 0]
    trow = tile_row[0, 0]
    tcol = tile_col[0, 0]
    live = tile_live[0, 0]
    trows = block_rows // TILE
    tcols = col_nodes // TILE
    gathered = lax.all_gather(x_feat, "row", axis=1, tiled=True)
    prods = slot_products(vals, tcol, gathered, False)
    partial_value = place_tiles(prods, trow, live, trows)
    agg = lax.psum_scatter(
        partial_value.astype(jnp.bfloat16), "col", scatter_dimension=0, tiled=True
    )
    layer_out = jnp.dot(agg, weight, preferred_element_type=jnp.float32).astype(jnp.bfloat16)
    d_agg = lax.dot_general(
        d_out, weight, (((1,), (1,)), ((), ())), preferred_element_type=jnp.float32
    ).astype(jnp.bfloat16)
    grad_term = lax.dot_general(
        agg, d_out, (((0,), (0,)), ((), ())), preferred_element_type=jnp.float32
    )
    scale = 1.0 / math.sqrt(block_rows * n_row)
    weight_grad = lax.psum(grad_term, ("row", "col")) * scale
    grad_block = lax.all_gather(d_agg, "col", axis=0, tiled=True)
    back_prods = slot_products(vals, trow, grad_block, True)
    back_partial = place_tiles(back_prods, tcol, live, tcols)
    feat_grad = lax.psum_scatter(
        back_partial.astype(jnp.bfloat16), "row", scatter_dimension=1, tiled=True
    )
    return (layer_out, weight_grad, feat_grad)


def solution(mesh):
    placed = (
        P("col", "row"),
        P(),
        P("row", "col", None, None, None),
        P("row", "col", None),
        P("row", "col", None),
        P("row", "col", None),
        P(("row", "col"), None),
    )
    return jax.shard_map(
        local,
        mesh=mesh,
        in_specs=placed,
        out_specs=(P(("row", "col"), None), P(), P("col", "row")),
        check_vma=False,
    )
```

profile of v0, /device:TPU:1, one launch (start us, length us, event | category | flops | bytes accessed | tf_op | source)
XLA Modules:
  0.0 595.7 jit_solution(4015984636249047431)
XLA Ops:
  7.2 0.7 all-gather.3.cloned.1.call-update
  8.0 1.9 convolution_convert_fusion.2
  10.0 0.7 fusion.26
  10.6 0.7 compare_and_fusion.1
  11.9 67.5 %all-gather.3.cloned.1.call-done = bf16[2048,256]{0,1:T(8,128)(2,1)} async-done(((bf16[2048,16]{0,1:T(8,128)(2,1)}), bf16[2048,256]{0,1:T(8,128)(2,1)}) %all-gather.3.cloned.1.call-update) | async-done | bytes 1048592 | tf_op jit(solution)/shard_map/all_gather | solution.py:39
  79.4 2.3 copy.14
  81.7 7.2 %gather_fusion = bf16[96,128,256]{2,1,0:T(8,128)(2,1)} fusion(bf16[16,128,256]{2,1,0:T(8,128)(2,1)} %bitcast.43, s32[1024]{0:T(1024)S(1)} %pad_clamp_fusion.1), kind=kCustom, calls=%fused_computation | custom fusion | bytes 12583296 | tf_op jit(solution)/shard_map/jit(_take)/gather | solution.py:14
  88.9 7.5 %fusion.6 = bf16[96,128,256]{1,2,0:T(8,128)(2,1)} fusion(bf16[96,128,256]{2,1,0:T(8,128)(2,1)} %gather_fusion, pred[96]{0:T(512)(128)(4,1)S(1)} %compare_and_fusion.1, bf16[1,1,96,128,128]{4,3,2,1,0:T(8,128)(2,1)S(1)} %copy-done), kind=kOutput, calls=%fused_computation.8 | convolution fusion | flops 808452096 | bytes 15728736 | tf_op jit(solution)/shard_map/sij,sjf->sif/dot_general | solution.py:17
  96.4 8.9 %copy.16 = bf16[96,128,256]{2,0,1:T(8,128)(2,1)} copy(bf16[96,128,256]{1,2,0:T(8,128)(2,1)} %fusion.6) | data formatting | bytes 12582912 | tf_op jit(solution)/shard_map/sij,sjf->sif/dot_general | solution.py:17
  105.3 3.8 convolution_convert_fusion
  109.0 2.5 copy.17
  111.6 41.0 %all-gather.5.cloned.1.call-done = bf16[4096,256]{1,0:T(8,128)(2,1)} async-done(((bf16[128,256]{1,0:T(8,128)(2,1)}), bf16[4096,256]{1,0:T(8,128)(2,1)}) %all-gather.5.cloned.1.call-update) | async-done | bytes 2097168 | tf_op jit(solution)/shard_map/all_gather | solution.py:54
  152.6 7.6 %gather_fusion.1 = bf16[96,128,256]{2,1,0:T(8,128)(2,1)} fusion(bf16[32,128,256]{2,1,0:T(8,128)(2,1)} %bitcast.44, s32[1024]{0:T(1024)S(1)} %pad_clamp_fusion), kind=kCustom, calls=%fused_computation.1 | custom fusion | bytes 12583296 | tf_op jit(solution)/shard_map/jit(_take)/gather | solution.py:14
  160.2 7.5 %fusion.9 = bf16[96,128,256]{1,2,0:T(8,128)(2,1)} fusion(bf16[96,128,256]{2,1,0:T(8,128)(2,1)} %gather_fusion.1, pred[96]{0:T(512)(128)(4,1)S(1)} %compare_and_fusion, bf16[1,1,96,128,128]{4,3,2,1,0:T(8,128)(2,1)S(1)} %copy-done), kind=kOutput, calls=%fused_computation.9 | convolution fusion | flops 808452096 | bytes 15728736 | tf_op jit(solution)/shard_map/sji,sjf->sif/dot_general | solution.py:16
  167.7 9.0 %copy.19 = bf16[96,128,256]{2,0,1:T(8,128)(2,1)} copy(bf16[96,128,256]{1,2,0:T(8,128)(2,1)} %fusion.9) | data formatting | bytes 12582912 | tf_op jit(solution)/shard_map/sji,sjf->sif/dot_general | solution.py:16
  176.7 75.2 %reduce-scatter.5.cloned.1.call-done = bf16[128,256]{1,0:T(8,128)(2,1)} async-done(((bf16[4096,256]{1,0:T(8,128)(2,1)}), bf16[128,256]{1,0:T(8,128)(2,1)}) %reduce-scatter.5.cloned.1.call-update) | async-done | bytes 65552 | tf_op jit(solution)/shard_map/reduce_scatter | solution.py:42
  251.9 1.8 fusion.30
  253.7 3.7 convolution_convert_fusion.1
  257.5 1.4 copy.20
  258.8 2.3 copy.24
  261.2 0.8 convolution_convert_fusion.3
  261.9 262.7 %all-reduce.2.cloned.1.call-done = f32[256,256]{1,0:T(8,128)} async-done(((f32[256,256]{1,0:T(8,128)}), f32[256,256]{1,0:T(8,128)}) %all-reduce.2.cloned.1.call-update) | async-done | bytes 262160 | tf_op jit(solution)/shard_map/psum | solution.py:53
  524.6 1.7 broadcast_multiply_fusion
  526.3 62.9 %reduce-scatter.7.cloned.1.call-done = bf16[16,2048]{1,0:T(8,128)(2,1)} async-done(((bf16[256,2048]{1,0:T(8,128)(2,1)}), bf16[16,2048]{1,0:T(8,128)(2,1)}) %reduce-scatter.7.cloned.1.call-update) | async-done | bytes 65552
  (26 shorter events, 1.0 us)
Async XLA Ops:
  7.2 81.7 %copy-start = (bf16[1,1,96,128,128]{4,3,2,1,0:T(8,128)(2,1)S(1)}, bf16[1,1,96,128,128]{4,3,2,1,0:T(8,128)(2,1)}, u32[]{:S(2)}) copy-start(bf16[1,1,96,128,128]{4,3,2,1,0:T(8,128)(2,1)} %param.9) | copy-start | bytes 9437188
  7.2 72.2 %all-gather.3.cloned.1.call-start = ((), (), s32[]{:S(2)}) async-start(), calls=%async_computation.2 | async-start | bytes 1114112 | tf_op jit(solution)/shard_map/all_gather | solution.py:39
  7.9 144.7 %all-gather.5.cloned.1.call-start = ((), (), s32[]{:S(2)}) async-start(), calls=%async_computation.5 | async-start | bytes 2162688 | tf_op jit(solution)/shard_map/all_gather | solution.py:54
  9.9 242.0 %reduce-scatter.5.cloned.1.call-start = ((), (), s32[]{:S(2)}) async-start(), calls=%async_computation.3 | async-start | bytes 2162688 | tf_op jit(solution)/shard_map/reduce_scatter | solution.py:42
  96.4 8.9 %copy-start.4 = (s32[1,1,96]{2,1,0:T(1,128)S(1)}, s32[1,1,96]{2,1,0:T(1,128)}, u32[]{:S(2)}) copy-start(s32[1,1,96]{2,1,0:T(1,128)} %param.10) | copy-start | bytes 1156
  111.6 413.1 %all-reduce.2.cloned.1.call-start = ((), (), s32[]{:S(2)}) async-start(), calls=%async_computation.4 | async-start | bytes 524288 | tf_op jit(solution)/shard_map/psum | solution.py:53
  167.7 84.2 %copy-start.2 = (bf16[128,256]{1,0:T(8,128)(2,1)S(1)}, bf16[128,256]{1,0:T(8,128)(2,1)}, u32[]{:S(2)}) copy-start(bf16[128,256]{1,0:T(8,128)(2,1)} %param.13) | copy-start | bytes 196612
  167.7 86.1 %copy-start.5 = (s32[1,1,96]{2,1,0:T(1,128)S(1)}, s32[1,1,96]{2,1,0:T(1,128)}, u32[]{:S(2)}) copy-start(s32[1,1,96]{2,1,0:T(1,128)} %param.11) | copy-start | bytes 1156
  253.7 335.5 %reduce-scatter.7.cloned.1.call-start = ((), (), s32[]{:S(2)}) async-start(), calls=%async_computation.6 | async-start | bytes 1114112
  253.7 7.4 %copy-start.1 = (bf16[256,256]{1,0:T(8,128)(2,1)S(1)}, bf16[256,256]{1,0:T(8,128)(2,1)}, u32[]{:S(2)}) copy-start(bf16[256,256]{1,0:T(8,128)(2,1)} %param.8) | copy-start | bytes 393220
  253.7 7.4 %copy-start.3 = (bf16[128,256]{1,0:T(8,128)(2,1)S(1)}, bf16[128,256]{1,0:T(8,128)(2,1)}, u32[]{:S(2)}) copy-start(bf16[128,256]{1,0:T(8,128)(2,1)} %reduce-scatter.5.cloned.1.call-done) | copy-start | bytes 196612
Sparse Core Ops, SparseCore 0:
  10.1 69.2 all-gather.2
  83.1 69.4 all-gather.4
  157.0 94.8 reduce-scatter.4
  257.3 267.2 all-reduce.1
  528.1 61.0 reduce-scatter.6
where the time goes:
time: 607 us; the launch traced here: 596 us
  waiting for transfers between devices  510 us (84%)
  local copies, waits for them, and re-layouts  41.1 us (7%)
  matrix products  26.9 us (4%)
  between operations  13.9 us (2%)
    psum x1, waiting for transfers between devices, local(): weight_grad = lax.psum(grad_term, ('row', 'col')) * scale  263 us
    reduce_scatter x1, waiting for transfers between devices, local(): lax.psum_scatter(partial_value.astype(jnp.bfloat16), 'col', scatter_dimen...  75.2 us
    all_gather x1, waiting for transfers between devices, local(): gathered = lax.all_gather(x_feat, 'row', axis=1, tiled=True)  67.5 us
    unnamed x6, waiting for transfers between devices  63.6 us
    all_gather x1, waiting for transfers between devices, local(): grad_block = lax.all_gather(d_agg, 'col', axis=0, tiled=True)  41 us
    gather x2, local copies, waits for them, and re-layouts, slot_products(): picked = jnp.take(ftiles, index, axis=0)  14.8 us
  transfers between devices with their start and end apart: 5, of which 5 were waited for; matrix products, arithmetic and copies ran while one was open for 12% of the time, Pallas kernels for 0%

commit v1 on v0

v1 whole, which is shorter than its diff:
```python
import functools
import math

import jax
import jax.numpy as jnp
from jax import lax
from jax.experimental import pallas as pl
from jax.experimental.pallas import tpu as pltpu
from jax.sharding import PartitionSpec as P

TILE = 128
F = 256
NZ, NYL = 8, 2
NYH, NX, NK = 4, 4, 2
N_ROW, N_COL = NZ * NYL, NYH * NX * NK
SLOTS = 96
TR, TC = 32, 16
BF = jnp.bfloat16
F32 = jnp.float32
MESH = pl.DeviceIdType.MESH


def place():
    row, col = lax.axis_index("row"), lax.axis_index("col")
    return row // NYL, row % NYL, col // (NX * NK), (col // NK) % NX, col % NK


class Wire:
    def __init__(self, send, recv):
        self.send, self.recv, self.used, self.started = send, recv, 0, []

    def slot(self):
        self.used += 1
        return self.used - 1

    def start(self, slot, src, dst, device):
        copy = pltpu.make_async_remote_copy(
            src_ref=src, dst_ref=dst, send_sem=self.send.at[slot], recv_sem=self.recv.at[slot],
            device_id=device, device_id_type=MESH)
        copy.start()
        self.started.append(copy)

    def landed(self, slot, dst, device):
        pltpu.make_async_remote_copy(
            src_ref=dst, dst_ref=dst, send_sem=self.send.at[slot], recv_sem=self.recv.at[slot],
            device_id=device, device_id_type=MESH).wait_recv()

    def drain(self):
        for copy in self.started:
            copy.wait_send()


def devices_around():
    z, yl, yh, x, k = place()

    def at(dz=0, dyl=0, dyh=0, dx=0, dk=0):
        row = ((z + dz) % NZ) * NYL + (yl + dyl) % NYL
        col = (((yh + dyh) % NYH) * NX + (x + dx) % NX) * NK + (k + dk) % NK
        return row, col

    return at


N_GATHER = 1 + 16 + 4 + 16 + 16


def gather_kernel(x_ref, d_ref, xg, dg, send, recv):
    z, yl, yh, x, k = place()
    at = devices_around()
    me = at()
    wire = Wire(send, recv)
    zdev = {1: at(dz=1), -1: at(dz=-1)}
    xdev = {1: at(dx=1), -1: at(dx=-1)}
    ydev = {1: at(dyh=1), -1: at(dyh=-1)}
    sib, ylo = at(dk=1), at(dyl=1)
    barrier = pltpu.get_barrier_semaphore()
    around = [zdev[1], zdev[-1], xdev[1], xdev[-1], ydev[1], ydev[-1], sib, ylo]
    for device in around:
        pl.semaphore_signal(barrier, inc=1, device_id=device, device_id_type=MESH)
    pl.semaphore_wait(barrier, len(around))

    ys = wire.slot()
    zs = {(d, s, u): wire.slot() for d in (1, -1) for s in (1, 2, 3, 4) for u in (0, 1)}
    half = {1: pl.ds(0, TC // 2), -1: pl.ds(TC // 2, TC // 2)}

    def xchunk(dz, u):
        return xg.at[at(dz=dz, dyl=u)[0]]

    def xpart(dz, u, d, s):
        ref = xchunk(dz, u)
        return ref.at[half[d]] if s == 4 else ref

    def z_send(d, s, u, src=None):
        dst = xpart(-d * (s - 1), u, d, s)
        wire.start(zs[d, s, u], dst if src is None else src, dst, zdev[d])

    def z_landed(d, s, u):
        wire.landed(zs[d, s, u], xpart(-d * s, u, d, s), zdev[-d])

    def piece(j, dx=0, dk=0):
        return dg.at[at(dyh=j, dx=dx, dk=dk)[1]]

    rows = {1: pl.ds(0, TILE // 2), -1: pl.ds(TILE // 2, TILE // 2)}
    y1 = {d: wire.slot() for d in (1, -1)}
    y2 = {d: wire.slot() for d in (1, -1)}
    x1 = {(d, j): wire.slot() for d in (1, -1) for j in range(4)}
    x2 = {(d, j): wire.slot() for d in (1, -1) for j in range(4)}
    ks = {(j, dx): wire.slot() for j in range(4) for dx in range(4)}

    def to_x(j, src=None):
        for d in (1, -1):
            wire.start(x1[d, j], piece(j) if src is None else src, piece(j), xdev[d])

    def to_sib(j, dx, src=None):
        wire.start(ks[j, dx % 4], piece(j, dx) if src is None else src, piece(j, dx), sib)

    def x1_landed(j):
        for d in (1, -1):
            wire.landed(x1[d, j], piece(j, -d), xdev[-d])
            part = piece(j, -d).at[rows[d]]
            wire.start(x2[d, j], part, part, xdev[d])
            to_sib(j, -d)

    def x2_landed(j):
        for d in (1, -1):
            wire.landed(x2[d, j], piece(j, 2).at[rows[d]], xdev[-d])
        to_sib(j, 2)

    wire.start(ys, x_ref, xchunk(0, 0), ylo)
    for d in (1, -1):
        z_send(d, 1, 0, x_ref)
    for d in (1, -1):
        wire.start(y1[d], d_ref, piece(0), ydev[d])
    to_x(0, d_ref)
    to_sib(0, 0, d_ref)
    xg[me[0]] = x_ref[...]
    dg[me[1]] = d_ref[...]

    wire.landed(ys, xchunk(0, 1), ylo)
    for d in (1, -1):
        z_send(d, 1, 1)
    for d in (1, -1):
        wire.landed(y1[d], piece(-d), ydev[-d])
        part = piece(-d).at[rows[d]]
        wire.start(y2[d], part, part, ydev[d])
        to_x(-d % 4)
        to_sib(-d % 4, 0)
    for u in (0, 1):
        for d in (1, -1):
            z_landed(d, 1, u)
            z_send(d, 2, u)
    x1_landed(0)
    for d in (1, -1):
        wire.landed(y2[d], piece(2).at[rows[d]], ydev[-d])
    to_x(2)
    to_sib(2, 0)
    x1_landed(3)
    x1_landed(1)
    for u in (0, 1):
        for d in (1, -1):
            z_landed(d, 2, u)
            z_send(d, 3, u)
    x2_landed(0)
    x1_landed(2)
    x2_landed(3)
    x2_landed(1)
    for u in (0, 1):
        for d in (1, -1):
            z_landed(d, 3, u)
            z_send(d, 4, u)
    x2_landed(2)
    for u in (0, 1):
        for d in (1, -1):
            z_landed(d, 4, u)
    for j in range(4):
        for dx in range(4):
            wire.landed(ks[j, dx], piece(j, dx, 1), sib)
    wire.drain()


def gather(xt, d_out):
    vmem = pl.BlockSpec(memory_space=pltpu.VMEM)
    return pl.pallas_call(
        gather_kernel,
        out_shape=(
            jax.ShapeDtypeStruct((N_ROW, TC, F // N_ROW, TILE), BF),
            jax.ShapeDtypeStruct((N_COL, TILE, F), BF),
        ),
        in_specs=[vmem] * 2,
        out_specs=(vmem, vmem),
        scratch_shapes=[pltpu.SemaphoreType.DMA((N_GATHER,)), pltpu.SemaphoreType.DMA((N_GATHER,))],
        compiler_params=pltpu.CompilerParams(
            collective_id=0, has_side_effects=True, vmem_limit_bytes=24 << 20),
        name="gather",
    )(xt, d_out)


UNROLL = 8


def cell_kernel(trow, tcol, live, vals, xg, dg, w, pt, bt, g, acc_p, acc_b, gt):
    acc_p[...] = jnp.zeros_like(acc_p)
    acc_b[...] = jnp.zeros_like(acc_b)
    contract = (((1,), (1,)), ((), ()))

    def forward(i, carry):
        for v in range(UNROLL):
            s = i * UNROLL + v
            target = jnp.where(live[s] > 0, trow[s], TR)
            xt = xg[:, tcol[s]].reshape(F, TILE)
            acc_p[target] += lax.dot_general(xt, vals[s], contract, preferred_element_type=F32)
        return carry

    lax.fori_loop(0, SLOTS // UNROLL, forward, 0)

    def grads(i, carry):
        for v in range(UNROLL):
            t = i * UNROLL + v
            gt[t] = lax.dot_general(w[...], dg[t], contract, preferred_element_type=F32).astype(BF)
        return carry

    lax.fori_loop(0, TR // UNROLL, grads, 0)

    def backward(i, carry):
        for v in range(UNROLL):
            s = i * UNROLL + v
            target = jnp.where(live[s] > 0, tcol[s], TC)
            acc_b[target] += jnp.dot(gt[trow[s]], vals[s], preferred_element_type=F32)
        return carry

    lax.fori_loop(0, SLOTS // UNROLL, backward, 0)

    def finish(i, total):
        for v in range(UNROLL):
            t = i * UNROLL + v
            tile = acc_p[t].astype(BF)
            pt[t] = tile
            total += jnp.dot(tile, dg[t], preferred_element_type=F32)
        return total

    total = lax.fori_loop(0, TR // UNROLL, finish, jnp.zeros((F, F), F32)).astype(BF)
    for q in range(N_COL):
        a, h = q // 2, q % 2
        g[q] = total[a * 16:(a + 1) * 16, h * TILE:(h + 1) * TILE]

    def spread(i, carry):
        bt[:, i] = acc_b[i].astype(BF).reshape(N_ROW, F // N_ROW, TILE)
        return carry

    lax.fori_loop(0, TC, spread, 0)


def cell(trow, tcol, live, vals, xg, dg, w):
    vmem = pl.BlockSpec(memory_space=pltpu.VMEM)
    smem = pl.BlockSpec(memory_space=pltpu.SMEM)
    return pl.pallas_call(
        cell_kernel,
        out_shape=(
            jax.ShapeDtypeStruct((N_COL, F, TILE), BF),
            jax.ShapeDtypeStruct((N_ROW, TC, F // N_ROW, TILE), BF),
            jax.ShapeDtypeStruct((N_COL, 16, TILE), BF),
        ),
        in_specs=[smem] * 3 + [vmem] * 4,
        out_specs=(vmem, vmem, vmem),
        scratch_shapes=[
            pltpu.VMEM((TR + 1, F, TILE), F32),
            pltpu.VMEM((TC + 1, F, TILE), F32),
            pltpu.VMEM((TR, F, TILE), BF),
        ],
        compiler_params=pltpu.CompilerParams(vmem_limit_bytes=40 << 20),
        name="cell",
    )(trow, tcol, live, vals, xg, dg, w)


N_REDUCE = 4 + 8 + 8 + 2 + 2 + 16 + 1


def total_of(refs):
    out = refs[0][...].astype(F32)
    for ref in refs[1:]:
        out += ref[...].astype(F32)
    return out.astype(BF)


def reduce_kernel(scale, pt, bt, g, w, layer, feat, wgrad,
                  gall, core_in, c, x1p, x1m, x2p, x2m, dsum, y1p, y1m, y2p, y2m,
                  bp, bm, e, ylr, g_in, g_sum, g_row, g_tot, send, recv, gsend, grecv):
    z, yl, yh, x, k = place()
    at = devices_around()
    row, col = at()
    wire = Wire(send, recv)
    zdev = {1: at(dz=1), -1: at(dz=-1)}
    xdev = {1: at(dx=1), -1: at(dx=-1)}
    ydev = {1: at(dyh=1), -1: at(dyh=-1)}
    sib, ylo = at(dk=1), at(dyl=1)
    barrier = pltpu.get_barrier_semaphore()

    def greet_col(o, carry):
        pl.semaphore_signal(barrier, inc=1, device_id=(row, (col + o) % N_COL), device_id_type=MESH)
        return carry

    def greet_row(o, carry):
        pl.semaphore_signal(barrier, inc=1, device_id=((row + o) % N_ROW, col), device_id_type=MESH)
        return carry

    lax.fori_loop(1, N_COL, greet_col, 0)
    lax.fori_loop(1, N_ROW, greet_row, 0)
    pl.semaphore_wait(barrier, N_COL + N_ROW - 2)

    x1b, x2b = {1: x1p, -1: x1m}, {1: x2p, -1: x2m}
    y1b, y2b = {1: y1p, -1: y1m}, {1: y2p, -1: y2m}
    bb = {1: bp, -1: bm}
    near = {1: pl.ds(0, TILE), -1: pl.ds(TILE, TILE)}
    far = {1: near[-1], -1: near[1]}
    bnear = {1: pl.ds(0, TC // 2), -1: pl.ds(TC // 2, TC // 2)}
    bfar = {1: bnear[-1], -1: bnear[1]}

    def yy(j):
        return (yh + j) % NYH

    order = (2, 1, 3, 0)
    cs = {j: wire.slot() for j in order}
    xs1 = {(d, j): wire.slot() for d in (1, -1) for j in order}
    xs2 = {(d, j): wire.slot() for d in (1, -1) for j in order}
    ys1 = {d: wire.slot() for d in (1, -1)}
    ys2 = {d: wire.slot() for d in (1, -1)}
    bs = {(d, s, u): wire.slot() for d in (1, -1) for s in (0, 1, 2, 3) for u in (0, 1)}
    yls = wire.slot()

    def bt_at(dz, u):
        return bt.at[at(dz=dz, dyl=u)[0]]

    def b_send(d, s, u):
        if s == 0:
            wire.start(bs[d, s, u], bt_at(4, u).at[bnear[d]], bb[d].at[0, u, bnear[d]], zdev[d])
        else:
            wire.start(bs[d, s, u], bb[d].at[s - 1, u], bb[d].at[s, u], zdev[d])

    def b_add(d, s, u):
        own = bt_at(d * (3 - s), u)
        if s == 0:
            landing = bb[d].at[0, u, bnear[d]]
            bb[d][0, u, bfar[d]] = own[bfar[d]]
            wire.landed(bs[d, s, u], landing, zdev[-d])
            bb[d][0, u, bnear[d]] = total_of([landing, own.at[bnear[d]]])
        else:
            landing = bb[d].at[s, u]
            wire.landed(bs[d, s, u], landing, zdev[-d])
            bb[d][s, u] = total_of([landing, own])
        b_send(d, s + 1, u)

    def b_step(s):
        for u in (1, 0):
            for d in (1, -1):
                b_add(d, s, u)

    for j in order:
        wire.start(cs[j], pt.at[yy(j), :, 1 - k], core_in.at[yy(j)], sib)
    for u in (1, 0):
        for d in (1, -1):
            b_send(d, 0, u)

    def g_out(o, carry):
        to = (col + o) % N_COL
        pltpu.make_async_remote_copy(
            src_ref=g.at[to], dst_ref=g_in.at[o - 1], send_sem=gsend.at[0], recv_sem=grecv.at[0],
            device_id=(row, to), device_id_type=MESH).start()
        return carry

    lax.fori_loop(1, N_COL, g_out, 0)

    for j in order:
        wire.landed(cs[j], core_in.at[yy(j)], sib)

        def add(i, carry):
            c[yy(j), i] = total_of([pt.at[yy(j), i, k], core_in.at[yy(j), i]])
            return carry

        lax.fori_loop(0, NX, add, 0)
        for d in (1, -1):
            wire.start(xs1[d, j], c.at[yy(j), (x + 2) % NX, near[d]], x1b[d].at[j, near[d]], xdev[d])

    b_step(0)

    pltpu.make_async_copy(g_in, g_in, grecv.at[0]).wait()
    g_sum[...] = (jnp.sum(g_in[...].astype(F32), axis=0) + g[col].astype(F32)).astype(BF)

    def g_rows(o, carry):
        to = (row + o) % N_ROW
        pltpu.make_async_remote_copy(
            src_ref=g_sum, dst_ref=g_row.at[o - 1], send_sem=gsend.at[1], recv_sem=grecv.at[1],
            device_id=(to, col), device_id_type=MESH).start()
        return carry

    lax.fori_loop(1, N_ROW, g_rows, 0)

    for j in order:
        for d in (1, -1):
            own = c.at[yy(j), (x + d) % NX]
            x1b[d][j, far[d]] = own[far[d]]
            landing = x1b[d].at[j, near[d]]
            wire.landed(xs1[d, j], landing, xdev[-d])
            x1b[d][j, near[d]] = total_of([landing, own.at[near[d]]])
            wire.start(xs2[d, j], x1b[d].at[j], x2b[d].at[j], xdev[d])

    b_step(1)

    pltpu.make_async_copy(g_row, g_row, grecv.at[1]).wait()
    g_tot[...] = (jnp.sum(g_row[...].astype(F32), axis=0) + g_sum[...].astype(F32)).astype(BF)
    gall[0] = g_tot[...]

    def g_back(o, carry):
        to = (col + o) % N_COL
        pltpu.make_async_remote_copy(
            src_ref=g_tot, dst_ref=gall.at[o], send_sem=gsend.at[2], recv_sem=grecv.at[2],
            device_id=(row, to), device_id_type=MESH).start()
        return carry

    lax.fori_loop(1, N_COL, g_back, 0)

    for j in order:
        for d in (1, -1):
            wire.landed(xs2[d, j], x2b[d].at[j], xdev[-d])
        dsum[j] = total_of([c.at[yy(j), x], x2p.at[j], x2m.at[j]])
        if j == 2:
            for d in (1, -1):
                wire.start(ys1[d], dsum.at[2, near[d]], y1b[d].at[near[d]], ydev[d])
        if j in (1, 3):
            d = 1 if j == 1 else -1
            y1b[d][far[d]] = dsum[j, far[d]]
            landing = y1b[d].at[near[d]]
            wire.landed(ys1[d], landing, ydev[-d])
            y1b[d][near[d]] = total_of([landing, dsum.at[j, near[d]]])
            wire.start(ys2[d], y1b[d], y2b[d], ydev[d])

    b_step(2)

    for d in (1, -1):
        wire.landed(ys2[d], y2b[d], ydev[-d])
    agg = total_of([dsum.at[0], y2p, y2m])
    layer[...] = lax.dot_general(
        agg, w[...], (((0,), (0,)), ((), ())), preferred_element_type=F32).astype(BF)

    for u in (1, 0):
        for d in (1, -1):
            wire.landed(bs[d, 3, u], bb[d].at[3, u], zdev[-d])
        e[u] = total_of([bt_at(0, u), bp.at[3, u], bm.at[3, u]])
        if u == 1:
            wire.start(yls, e.at[1], ylr, ylo)
    wire.landed(yls, ylr, ylo)
    feat[...] = total_of([e.at[0], ylr])

    others = gall.at[pl.ds(1, N_COL - 1)]
    pltpu.make_async_copy(others, others, grecv.at[2]).wait()
    for q in range(N_COL):
        a, h = q // 2, q % 2
        chunk = gall[(col - q + N_COL) % N_COL].astype(F32) * scale
        wgrad[a * 16:(a + 1) * 16, h * TILE:(h + 1) * TILE] = chunk
    pltpu.make_async_copy(g_in, g_in, gsend.at[0]).wait()
    pltpu.make_async_copy(g_row, g_row, gsend.at[1]).wait()
    pltpu.make_async_copy(others, others, gsend.at[2]).wait()
    wire.drain()


def reduce(pt, bt, g, w, scale):
    vmem = pl.BlockSpec(memory_space=pltpu.VMEM)
    return pl.pallas_call(
        functools.partial(reduce_kernel, scale),
        out_shape=(
            jax.ShapeDtypeStruct((TILE, F), BF),
            jax.ShapeDtypeStruct((TC, F // N_ROW, TILE), BF),
            jax.ShapeDtypeStruct((F, F), F32),
        ),
        in_specs=[vmem] * 4,
        out_specs=(vmem, vmem, vmem),
        scratch_shapes=[
            pltpu.VMEM((N_COL, 16, TILE), BF),
            pltpu.VMEM((NYH, NX, F, TILE), BF),
            pltpu.VMEM((NYH, NX, F, TILE), BF),
            pltpu.VMEM((NYH, F, TILE), BF),
            pltpu.VMEM((NYH, F, TILE), BF),
            pltpu.VMEM((NYH, F, TILE), BF),
            pltpu.VMEM((NYH, F, TILE), BF),
            pltpu.VMEM((NYH, F, TILE), BF),
            pltpu.VMEM((F, TILE), BF),
            pltpu.VMEM((F, TILE), BF),
            pltpu.VMEM((F, TILE), BF),
            pltpu.VMEM((F, TILE), BF),
            pltpu.VMEM((4, NYL, TC, F // N_ROW, TILE), BF),
            pltpu.VMEM((4, NYL, TC, F // N_ROW, TILE), BF),
            pltpu.VMEM((NYL, TC, F // N_ROW, TILE), BF),
            pltpu.VMEM((TC, F // N_ROW, TILE), BF),
            pltpu.VMEM((N_COL - 1, 16, TILE), BF),
            pltpu.VMEM((16, TILE), BF),
            pltpu.VMEM((N_ROW - 1, 16, TILE), BF),
            pltpu.VMEM((16, TILE), BF),
            pltpu.SemaphoreType.DMA((N_REDUCE,)),
            pltpu.SemaphoreType.DMA((N_REDUCE,)),
            pltpu.SemaphoreType.DMA((3,)),
            pltpu.SemaphoreType.DMA((3,)),
        ],
        compiler_params=pltpu.CompilerParams(
            collective_id=1, has_side_effects=True, vmem_limit_bytes=32 << 20),
        name="reduce",
    )(pt, bt, g, w)


def local(x_feat, weight, tile_vals, tile_row, tile_col, tile_live, d_out):
    nodes = d_out.shape[0] * N_COL * N_ROW
    xt = x_feat.reshape(TC, TILE, F // N_ROW).transpose(0, 2, 1)
    xg, dg = gather(xt, d_out)
    pt, bt, g = cell(tile_row[0, 0], tile_col[0, 0], tile_live[0, 0], tile_vals[0, 0], xg, dg, weight)
    scale = 1.0 / math.sqrt(nodes)
    layer, feat, wgrad = reduce(pt.reshape(NYH, NX, NK, F, TILE), bt, g, weight, scale)
    feat = feat.transpose(0, 2, 1).reshape(TC * TILE, F // N_ROW)
    return layer, wgrad, feat


def solution(mesh):
    placed = (
        P("col", "row"),
        P(),
        P("row", "col", None, None, None),
        P("row", "col", None),
        P("row", "col", None),
        P("row", "col", None),
        P(("row", "col"), None),
    )
    return jax.shard_map(
        local,
        mesh=mesh,
        in_specs=placed,
        out_specs=(P(("row", "col"), None), P(), P("col", "row")),
        check_vma=False,
    )
```

time: 607 us -> 89.2 us (0.15); the launches traced: 596 us -> 88 us
  waiting for transfers between devices: 510 us -> 0 us
  Pallas kernels: 0 us -> 78.9 us
  local copies, waits for them, and re-layouts: 41.1 us -> 8.4 us
  matrix products: 26.9 us -> 0 us
  between operations: 13.9 us -> 0.69 us
    psum x1 -> x0, waiting for transfers between devices: 263 us -> none  [local(): weight_grad = lax.psum(grad_term, ('row', 'col')) * scale]
    all_gather x2 -> x0, waiting for transfers between devices: 108 us -> none  [the longest x1 67.5 us: local(): gathered = lax.all_gather(x_feat, 'row', axis=1, tiled=True)]
    pallas_call x0 -> x3, Pallas kernels: none -> 78.9 us  [the longest x1 35.2 us: gather(): pl.pallas_call(gather_kernel, out_shape=(jax.ShapeDtypeStruct((N_ROW, TC,...]
    reduce_scatter x1 -> x0, waiting for transfers between devices: 75.2 us -> none  [local(): lax.psum_scatter(partial_value.astype(jnp.bfloat16), 'col', scatter_dimen...]
    unnamed x6 -> x0, waiting for transfers between devices: 63.6 us -> none
    dot_general x7 -> x0, matrix products: 26.9 us -> none  [the longest x2 7.5 us: place_tiles(): placed = jnp.einsum('ts,sif->tif', onehot, prods)]
    dot_general x2 -> x0, local copies, waits for them, and re-layouts: 17.9 us -> none  [the longest x1 8.99 us: slot_products(): jnp.einsum('sji,sjf->sif', vals, picked, preferred_element_type=jnp.float32)]
    gather x2 -> x0, local copies, waits for them, and re-layouts: 14.8 us -> none  [slot_products(): picked = jnp.take(ftiles, index, axis=0)]
  transfers between devices with their start and end apart: 5 -> 0, of which waited for: 5 -> 0; matrix products, arithmetic and copies ran while one was open for 12% -> 0% of each run, Pallas kernels for 0% -> 0%
where the time goes in v1:
time: 89.2 us; the launch traced here: 88 us
  Pallas kernels  78.9 us (88%)
  local copies, waits for them, and re-layouts  8.4 us (9%)
    pallas_call x1, Pallas kernels, gather(): pl.pallas_call(gather_kernel, out_shape=(jax.ShapeDtypeStruct((N_ROW, TC,...  35.2 us
    pallas_call x1, Pallas kernels, reduce(): pl.pallas_call(functools.partial(reduce_kernel, scale), out_shape=(jax.Sh...  31.8 us
    pallas_call x1, Pallas kernels, cell(): pl.pallas_call(cell_kernel, out_shape=(jax.ShapeDtypeStruct((N_COL, F, TI...  11.9 us
    unnamed x16, local copies, waits for them, and re-layouts  7.76 us

profile of v1, /device:TPU:1, one launch (start us, length us, event | category | flops | bytes accessed | tf_op | source)
XLA Modules:
  0.0 88.0 jit_solution(9163187080021035482)
XLA Ops:
  0.6 0.0 copy-start
  0.6 0.8 copy-done
  1.5 0.0 copy-start.3
  1.5 0.8 copy-done.3
  2.3 35.2 %gather.1 = (bf16[16,16,16,128]{3,2,1,0:T(8,128)(2,1)S(1)}, bf16[32,128,256]{2,1,0:T(8,128)(2,1)S(1)}) custom-call(bf16[16,16,128]{2,1,0:T(8,128)(2,1)S(1)} %bitcast_bitcast_fusion.x_ref, bf16[128,256]{1,0:T(8,128)(2,1)S(1)} %copy-done.3), custom_call_target="tpu_custom_call" | custom-call | tf_op jit(solution)/shard_map/gather/pallas_call | solution.py:183
  37.6 0.0 copy-start.1
  37.6 1.9 %copy-done.1 = bf16[1,1,96,128,128]{4,3,2,1,0:T(8,128)(2,1)S(1)} copy-done((bf16[1,1,96,128,128]{4,3,2,1,0:T(8,128)(2,1)S(1)}, bf16[1,1,96,128,128]{4,3,2,1,0:T(8,128)(2,1)}, u32[]{:S(2)}) %copy-start.1) | copy-done | bytes 3145752
  39.5 0.0 copy-start.2
  39.5 0.9 %copy-done.2 = bf16[256,256]{1,0:T(8,128)(2,1)S(1)} copy-done((bf16[256,256]{1,0:T(8,128)(2,1)S(1)}, bf16[256,256]{1,0:T(8,128)(2,1)}, u32[]{:S(2)}) %copy-start.2) | copy-done | bytes 131096
  40.4 0.0 copy-start.4
  40.4 0.7 copy-done.4
  41.0 0.0 copy-start.5
  41.0 0.7 copy-done.5
  41.7 0.0 copy-start.6
  41.7 0.7 copy-done.6
  42.4 11.9 %cell.1 = (bf16[32,256,128]{2,1,0:T(8,128)(2,1)S(1)}, bf16[16,16,16,128]{3,2,1,0:T(8,128)(2,1)S(1)}, bf16[32,16,128]{2,1,0:T(8,128)(2,1)S(1)}) custom-call(s32[96]{0:T(128)S(1)} %bitcast.20, s32[96]{0:T(128)S(1)} %bitcast.21, s32[96]{0:T(128)S(1)} %bitcast.22, bf16[96,128,128]{2,1,0:T(8,128)(2,1)S(1)} %bitcast.18, ...), custom_call_target="tpu_custom_call" | custom-call | tf_op jit(solution)/shard_map/cell/pallas_call | solution.py:256
  54.3 31.8 %reduce.1 = (bf16[128,256]{1,0:T(8,128)(2,1)S(1)}, bf16[16,16,128]{2,1,0:T(8,128)(2,1)S(1)}, f32[256,256]{1,0:T(8,128)S(1)}) custom-call(bf16[4,4,2,256,128]{4,3,2,1,0:T(8,128)(2,1)S(1)} %bitcast.19, bf16[16,16,16,128]{3,2,1,0:T(8,128)(2,1)S(1)} %get-tuple-element.14.bt, bf16[32,16,128]{2,1,0:T(8,128)(2,1)S(1)} %get-tuple-element.15.g, ...), custom_call_target="tpu_custom_call" | custom-call | tf_op jit(solution)/shard_map/reduce/pallas_call | solution.py:467
  86.0 0.6 copy_bitcast_fusion
  86.7 0.6 copy.18
  87.3 0.7 copy.19
  (1 shorter events, 0.0 us)
Async XLA Ops:
  0.6 0.8 copy-start
  1.5 0.8 copy-start.3
  37.6 1.9 %copy-start.1 = (bf16[1,1,96,128,128]{4,3,2,1,0:T(8,128)(2,1)S(1)}, bf16[1,1,96,128,128]{4,3,2,1,0:T(8,128)(2,1)}, u32[]{:S(2)}) copy-start(bf16[1,1,96,128,128]{4,3,2,1,0:T(8,128)(2,1)} %param.9) | copy-start | bytes 9437188
  39.5 0.9 %copy-start.2 = (bf16[256,256]{1,0:T(8,128)(2,1)S(1)}, bf16[256,256]{1,0:T(8,128)(2,1)}, u32[]{:S(2)}) copy-start(bf16[256,256]{1,0:T(8,128)(2,1)} %w.3) | copy-start | bytes 393220
  40.4 0.7 copy-start.4
  41.0 0.7 copy-start.5
  41.7 0.7 copy-start.6

commit v2 on v0

v2 whole, which is shorter than its diff:
```python
import functools
import math

import jax
import jax.numpy as jnp
from jax import lax
from jax.experimental import pallas as pl
from jax.experimental.pallas import tpu as pltpu
from jax.sharding import PartitionSpec as P

TILE = 128
F = 256
NZ, NYL = 8, 2
NYH, NX, NK = 4, 4, 2
N_ROW, N_COL = NZ * NYL, NYH * NX * NK
SLOTS = 96
TR, TC = 32, 16
BF = jnp.bfloat16
F32 = jnp.float32
MESH = pl.DeviceIdType.MESH


def place():
    row, col = lax.axis_index("row"), lax.axis_index("col")
    return row // NYL, row % NYL, col // (NX * NK), (col // NK) % NX, col % NK


class Wire:
    def __init__(self, send, recv):
        self.send, self.recv, self.used, self.started = send, recv, 0, []

    def slot(self):
        self.used += 1
        return self.used - 1

    def start(self, slot, src, dst, device):
        copy = pltpu.make_async_remote_copy(
            src_ref=src, dst_ref=dst, send_sem=self.send.at[slot], recv_sem=self.recv.at[slot],
            device_id=device, device_id_type=MESH)
        copy.start()
        self.started.append(copy)

    def landed(self, slot, dst, device):
        pltpu.make_async_remote_copy(
            src_ref=dst, dst_ref=dst, send_sem=self.send.at[slot], recv_sem=self.recv.at[slot],
            device_id=device, device_id_type=MESH).wait_recv()

    def drain(self):
        for copy in self.started:
            copy.wait_send()


def devices_around():
    z, yl, yh, x, k = place()

    def at(dz=0, dyl=0, dyh=0, dx=0, dk=0):
        row = ((z + dz) % NZ) * NYL + (yl + dyl) % NYL
        col = (((yh + dyh) % NYH) * NX + (x + dx) % NX) * NK + (k + dk) % NK
        return row, col

    return at


N_LINK = 1 + 16 + 3 + 12 + 16 + 4 + 12 + 3 + 16 + 1
UNROLL = 8
RUN = 32
NT = (((1,), (1,)), ((), ()))
TN = (((0,), (0,)), ((), ()))


def total_of(refs):
    out = refs[0][...].astype(F32)
    for ref in refs[1:]:
        out += ref[...].astype(F32)
    return out.astype(BF)


def sorted_rows(key, other, rows):
    shape = (TILE, TILE)
    lane = lax.broadcasted_iota(jnp.int32, shape, 1)
    down = lax.broadcasted_iota(jnp.int32, shape, 0)
    keys = jnp.broadcast_to(key, shape)
    mine = keys * TILE + lane
    theirs = mine.T
    rank = jnp.sum((mine < theirs).astype(jnp.int32), axis=1, keepdims=True)
    hot = rank == lane
    key_down = keys.T
    other_down = jnp.broadcast_to(other, shape).T
    for i, value in enumerate((down, other_down, key_down)):
        rows[i:i + 1, :] = jnp.sum(jnp.where(hot, value, 0), axis=0, keepdims=True)
    rows[3:4, :] = jnp.sum((key_down <= lane).astype(jnp.int32), axis=0, keepdims=True)


def layer_kernel(scale, x_in, w_in, vals_in, trow_in, tcol_in, live_in, d_in, layer, feat, wgrad,
                 wl, w, vals, idx, keys, meta_v, meta, xl, dl, xg, dg, runs, pt, bt,
                 core_in, c, xin, dsum, yin, b1, b2, b3, b4, bmid, e, ylr, g, g_in, g_part,
                 loads, send, recv, gsend, grecv):
    z, yl, yh, x, k = place()
    at = devices_around()
    row, col = at()
    wire = Wire(send, recv)
    zdev = {1: at(dz=1), -1: at(dz=-1)}
    sib, ylo = at(dk=1), at(dyl=1)
    barrier = pltpu.get_barrier_semaphore()

    m, n = col % (NX * NK), yh * NYL + yl

    def plane_x(o):
        return row, yh * (NX * NK) + (m + o) % 8

    def plane_y(o):
        there = (n + o) % 8
        return z * NYL + there % NYL, there // NYL * (NX * NK) + m

    def plane_z(o):
        return (z + o) % NZ * NYL + yl, col

    groups = (plane_x, plane_y, plane_z)
    for group in groups:
        for o in range(1, 8):
            pl.semaphore_signal(barrier, inc=1, device_id=group(o), device_id_type=MESH)

    load = [
        pltpu.make_async_copy(src, dst, loads.at[i])
        for i, (src, dst) in enumerate((
            (x_in, xl), (d_in, dl),
            (trow_in.at[0], idx.at[0]), (tcol_in.at[0], idx.at[1]), (live_in.at[0], idx.at[2]),
            (w_in, wl), (vals_in.at[0, 0], vals)))
    ]
    for copy in load:
        copy.start()
    load[0].wait()
    for t in range(TC):
        xg[1, 0, t] = xl[:, t * TILE:(t + 1) * TILE]
    load[1].wait()
    dg[col] = dl[...].astype(F32).T.astype(BF)
    pl.semaphore_wait(barrier, 7 * len(groups))

    ys = wire.slot()
    zs = {(d, s, u): wire.slot() for d in (1, -1) for s in (1, 2, 3, 4) for u in (0, 1)}
    half = {1: pl.ds(0, TC // 2), -1: pl.ds(TC // 2, TC // 2)}

    def xpart(dz, u, d, s):
        ref = xg.at[(dz + 1) % NZ, u]
        return ref.at[half[d]] if s == 4 else ref

    def z_send(d, s, u):
        hop = s if s < 3 else s - 2
        back = 0 if s < 3 else -2 * d
        wire.start(zs[d, s, u], xpart(back, u, d, s), xpart(-d * s, u, d, s), at(dz=hop * d))

    def z_landed(d, s, u):
        hop = s if s < 3 else s - 2
        wire.landed(zs[d, s, u], xpart(-d * s, u, d, s), at(dz=-hop * d))

    def z_first(u):
        for s in (2, 1):
            for d in (1, -1):
                z_send(d, s, u)

    def z_second(u):
        for d in (1, -1):
            z_landed(d, 2, u)
            for s in (3, 4):
                z_send(d, s, u)

    def z_third():
        for s in (1, 3, 4):
            for u in (0, 1):
                for d in (1, -1):
                    z_landed(d, s, u)

    def piece(j, dx=0, dk=0):
        return dg.at[at(dyh=j, dx=dx, dk=dk)[1]]

    dys = {o: wire.slot() for o in (1, 3, 2)}
    dxs = {(j, o): wire.slot() for j in range(4) for o in (1, 3, 2)}
    dks = {(j, dx): wire.slot() for j in range(4) for dx in range(4)}

    def d_to_x(j):
        for o in (1, 3, 2):
            wire.start(dxs[j, o], piece(j), piece(j), at(dx=o))
        wire.start(dks[j, 0], piece(j), piece(j), sib)

    def d_x_landed(j):
        for o in (1, 3, 2):
            part = piece(j, -o)
            wire.landed(dxs[j, o], part, at(dx=-o))
            wire.start(dks[j, -o % 4], part, part, sib)

    mine = xg.at[1, 0]
    z_first(0)
    wire.start(ys, mine, xg.at[1, 1], ylo)
    for o in (1, 3, 2):
        wire.start(dys[o], piece(0), piece(0), at(dyh=o))
    d_to_x(0)

    for copy in load[2:5]:
        copy.wait()
    keys[...] = jnp.full(keys.shape, TILE - 1, jnp.int32)
    for i in range(3):
        keys[i:i + 1, 0:SLOTS] = idx[i]
    alive = keys[2:3, :] > 0
    sorted_rows(jnp.where(alive, keys[0:1, :], TR), keys[1:2, :], meta_v.at[0:4])
    wire.landed(ys, xg.at[1, 1], ylo)
    z_first(1)
    sorted_rows(jnp.where(alive, keys[1:2, :], TC), keys[0:1, :], meta_v.at[4:8])
    to_scalars = pltpu.make_async_copy(meta_v, meta, loads.at[0])
    to_scalars.start()

    z_second(0)
    for o in (1, 3):
        wire.landed(dys[o], piece(-o), at(dyh=-o))
        d_to_x(-o % 4)
    z_second(1)
    wire.landed(dys[2], piece(2), at(dyh=2))
    d_to_x(2)
    d_x_landed(0)
    load[5].wait()
    for i in range(NZ):
        for u in (0, 1):
            b = (i * NYL + u) * (F // N_ROW)
            w[b:b + F // N_ROW, :] = wl[at(dz=i - 1, dyl=u)[0]]
    to_scalars.wait()
    load[6].wait()

    def run(base, source, contract):
        def step(i, acc):
            for v in range(RUN):
                s = i * RUN + v
                slot, other = meta[base, s], meta[base + 1, s]
                same = jnp.logical_and(s > 0, meta[base + 2, s] == meta[base + 2, jnp.maximum(s - 1, 0)])
                prod = lax.dot_general(source(other), vals[slot], contract, preferred_element_type=F32)
                acc = jnp.where(same, acc + prod, prod)
                runs[s] = acc.astype(BF)
            return acc
        lax.fori_loop(0, SLOTS // RUN, step, jnp.zeros((F, TILE), F32))

    def last_of(base, t):
        count = meta[base + 3, t]
        before = jnp.where(t > 0, meta[base + 3, jnp.maximum(t - 1, 0)], 0)
        value = runs[jnp.maximum(count - 1, 0)]
        return jnp.where(count > before, value, jnp.zeros_like(value))

    z_third()
    run(0, lambda i: xg[:, :, i].reshape(F, TILE), NT)

    order = (2, 1, 3, 0)
    near = (1, 3, 2)

    def yy(j):
        return (yh + j) % NYH

    cs = {j: wire.slot() for j in order}
    pxs = {(j, o): wire.slot() for j in order for o in near}
    pys = {o: wire.slot() for o in near}

    def fill(core):
        def one(i, carry):
            for v in range(NX):
                pt[i, v, core] = last_of(0, (i * NX + v) * NK + core)
            return carry
        return one

    lax.fori_loop(0, NYH, fill(1 - k), 0)
    for j in order:
        wire.start(cs[j], pt.at[yy(j), :, 1 - k], core_in.at[yy(j)], sib)

    for j in (3, 1, 2):
        d_x_landed(j)
    lax.fori_loop(0, NYH, fill(k), 0)

    b1s, b2s, b3s, b4s = ({(d, u): wire.slot() for d in (1, -1) for u in (0, 1)} for _ in range(4))
    side = {1: 0, -1: 1}
    yls = wire.slot()

    def bt_at(dz, u):
        return bt.at[(dz + 1) % NZ, u]

    def b_start():
        for u in (1, 0):
            for d in (1, -1):
                wire.start(b3s[d, u], bt_at(3 * d, u), b3.at[side[d], u], zdev[d])
                wire.start(b4s[d, u], bt_at(4, u).at[half[d]], b4.at[side[d], u], at(dz=2 * d))
        for u in (1, 0):
            for d in (1, -1):
                wire.start(b1s[d, u], bt_at(d, u), b1.at[side[d], u], zdev[d])

    def b_middle():
        for u in (1, 0):
            for d in (1, -1):
                wire.landed(b3s[d, u], b3.at[side[d], u], zdev[-d])
                wire.landed(b4s[d, u], b4.at[side[d], u], at(dz=-2 * d))
                mid, own = bmid.at[side[d], u], bt_at(2 * d, u)
                mid[half[-d]] = total_of([own.at[half[-d]], b3.at[side[d], u, half[-d]]])
                mid[half[d]] = total_of([own.at[half[d]], b3.at[side[d], u, half[d]], b4.at[side[d], u]])
                wire.start(b2s[d, u], mid, b2.at[side[d], u], at(dz=2 * d))

    for j in order:
        wire.landed(cs[j], core_in.at[yy(j)], sib)

        def add(i, carry):
            c[yy(j), i] = total_of([pt.at[yy(j), i, k], core_in.at[yy(j), i]])
            return carry

        lax.fori_loop(0, NX, add, 0)
        for o in near:
            wire.start(pxs[j, o], c.at[yy(j), (x + o) % NX], xin.at[o - 1, j], at(dx=o))

    def spread(i, carry):
        for v in range(UNROLL):
            t = i * UNROLL + v
            term = jnp.dot(w[...], last_of(4, t), preferred_element_type=F32)
            bt[:, :, t] = term.astype(BF).reshape(NZ, NYL, F // N_ROW, TILE)
        return carry

    for j in (0, 3, 1, 2):
        for dx in range(4):
            wire.landed(dks[j, dx], piece(j, dx, 1), sib)

    run(4, lambda i: dg[i], (((1,), (0,)), ((), ())))
    lax.fori_loop(0, TC // UNROLL, spread, 0)
    b_start()

    def grad_term(i, total):
        for v in range(UNROLL):
            total += lax.dot_general(
                pt[i, v // NK, v % NK], dg[i * UNROLL + v], NT, preferred_element_type=F32)
        return total

    total = lax.fori_loop(0, TR // UNROLL, grad_term, jnp.zeros((F, F), F32)).astype(BF)
    for i in range(NZ):
        for u in (0, 1):
            b, a = (i * NYL + u) * 16, at(dz=i - 1, dyl=u)[0]
            for h in (0, 1):
                g[2 * a + h] = total[b:b + 16, h * TILE:(h + 1) * TILE]

    def g_exchange(stage, group, source):
        for o in range(1, 8):
            pltpu.make_async_remote_copy(
                src_ref=source(o), dst_ref=g_in.at[stage, o - 1],
                send_sem=gsend.at[stage], recv_sem=grecv.at[stage],
                device_id=group(o), device_id_type=MESH).start()

    def g_landed(stage):
        landing = g_in.at[stage, pl.ds(0, 7)]
        pltpu.make_async_copy(landing, landing, grecv.at[stage]).wait()

    def g_add(stage, own):
        g_landed(stage)
        g_part[stage] = (jnp.sum(g_in[stage, 0:7].astype(F32), axis=0) + own[...].astype(F32)).astype(BF)

    g_exchange(0, plane_x, lambda o: g.at[pl.ds((m + o) % 8 * 4, 4)])

    def p_x_landed(j):
        for o in near:
            wire.landed(pxs[j, o], xin.at[o - 1, j], at(dx=-o))
        dsum[j] = total_of([c.at[yy(j), x], xin.at[0, j], xin.at[1, j], xin.at[2, j]])
        if j:
            wire.start(pys[j], dsum.at[j], yin.at[j - 1], at(dyh=j))

    p_x_landed(2)
    b_middle()
    p_x_landed(1)

    g_add(0, g.at[pl.ds(m * 4, 4)])
    g_exchange(1, plane_y, lambda o: g_part.at[0])

    p_x_landed(3)

    g_add(1, g_part.at[0])
    g_exchange(2, plane_z, lambda o: g_part.at[1])

    p_x_landed(0)

    g_add(2, g_part.at[1])
    g_exchange(3, plane_x, lambda o: g_part.at[2])

    for u in (1, 0):
        for d in (1, -1):
            wire.landed(b1s[d, u], b1.at[side[d], u], zdev[-d])
            wire.landed(b2s[d, u], b2.at[side[d], u], at(dz=-2 * d))
        e[u] = total_of([bt_at(0, u), b1.at[0, u], b1.at[1, u], b2.at[0, u], b2.at[1, u]])
        if u == 1:
            wire.start(yls, e.at[1], ylr, ylo)

    for o in near:
        wire.landed(pys[o], yin.at[o - 1], at(dyh=-o))
    agg = total_of([dsum.at[0], yin.at[0], yin.at[1], yin.at[2]])
    layer[...] = lax.dot_general(agg, w[...], TN, preferred_element_type=F32).astype(BF)

    g_landed(3)
    g_in[3, 7] = g_part[2]
    for q in range(N_COL):
        a, h = q // 2, q % 2
        chunk = g_in[3, (m - q // 4 + 7) % 8, q % 4].astype(F32) * scale
        wgrad[a * 16:(a + 1) * 16, h * TILE:(h + 1) * TILE] = chunk

    wire.landed(yls, ylr, ylo)
    mine = total_of([e.at[0], ylr])
    for t in range(TC):
        feat[:, t * TILE:(t + 1) * TILE] = mine[t]

    for stage in range(4):
        sent = g_in.at[stage, pl.ds(0, 7)]
        pltpu.make_async_copy(sent, sent, gsend.at[stage]).wait()
    wire.drain()


def layer_call(xt, w, vals, trow, tcol, live, d_out, scale):
    vmem = pl.BlockSpec(memory_space=pltpu.VMEM)
    here = pl.BlockSpec(memory_space=pltpu.HBM)
    fr = F // N_ROW
    ints = jnp.int32
    return pl.pallas_call(
        functools.partial(layer_kernel, scale),
        out_shape=(
            jax.ShapeDtypeStruct((TILE, F), BF),
            jax.ShapeDtypeStruct((fr, TC * TILE), BF),
            jax.ShapeDtypeStruct((F, F), F32),
        ),
        in_specs=[here] * 7,
        out_specs=(vmem, vmem, vmem),
        scratch_shapes=[
            pltpu.VMEM((N_ROW, F // N_ROW, F), BF),
            pltpu.VMEM((F, F), BF),
            pltpu.VMEM((SLOTS, TILE, TILE), BF),
            pltpu.VMEM((3, 1, SLOTS), ints),
            pltpu.VMEM((8, TILE), ints),
            pltpu.VMEM((8, TILE), ints),
            pltpu.SMEM((8, TILE), ints),
            pltpu.VMEM((fr, TC * TILE), BF),
            pltpu.VMEM((TILE, F), BF),
            pltpu.VMEM((NZ, NYL, TC, fr, TILE), BF),
            pltpu.VMEM((N_COL, F, TILE), BF),
            pltpu.VMEM((SLOTS, F, TILE), BF),
            pltpu.VMEM((NYH, NX, NK, F, TILE), BF),
            pltpu.VMEM((NZ, NYL, TC, fr, TILE), BF),
            pltpu.VMEM((NYH, NX, F, TILE), BF),
            pltpu.VMEM((NYH, NX, F, TILE), BF),
            pltpu.VMEM((NX - 1, NYH, F, TILE), BF),
            pltpu.VMEM((NYH, F, TILE), BF),
            pltpu.VMEM((NYH - 1, F, TILE), BF),
            pltpu.VMEM((2, NYL, TC, fr, TILE), BF),
            pltpu.VMEM((2, NYL, TC, fr, TILE), BF),
            pltpu.VMEM((2, NYL, TC, fr, TILE), BF),
            pltpu.VMEM((2, NYL, TC // 2, fr, TILE), BF),
            pltpu.VMEM((2, NYL, TC, fr, TILE), BF),
            pltpu.VMEM((NYL, TC, fr, TILE), BF),
            pltpu.VMEM((TC, fr, TILE), BF),
            pltpu.VMEM((N_COL, 16, TILE), BF),
            pltpu.VMEM((4, 8, 4, 16, TILE), BF),
            pltpu.VMEM((3, 4, 16, TILE), BF),
            pltpu.SemaphoreType.DMA((7,)),
            pltpu.SemaphoreType.DMA((N_LINK,)),
            pltpu.SemaphoreType.DMA((N_LINK,)),
            pltpu.SemaphoreType.DMA((4,)),
            pltpu.SemaphoreType.DMA((4,)),
        ],
        compiler_params=pltpu.CompilerParams(
            collective_id=0, has_side_effects=True, vmem_limit_bytes=56 << 20),
        name="graph_layer",
    )(xt, w.reshape(N_ROW, fr, F), vals, trow, tcol, live, d_out)


def local(x_feat, weight, tile_vals, tile_row, tile_col, tile_live, d_out):
    nodes = d_out.shape[0] * N_COL * N_ROW
    layer, feat, wgrad = layer_call(
        x_feat.T, weight, tile_vals, tile_row, tile_col, tile_live, d_out, 1.0 / math.sqrt(nodes))
    return layer, wgrad, feat.T


def solution(mesh):
    placed = (
        P("col", "row"),
        P(),
        P("row", "col", None, None, None),
        P("row", "col", None),
        P("row", "col", None),
        P("row", "col", None),
        P(("row", "col"), None),
    )
    return jax.shard_map(
        local,
        mesh=mesh,
        in_specs=placed,
        out_specs=(P(("row", "col"), None), P(), P("col", "row")),
        check_vma=False,
    )
```

time: 607 us -> 75.4 us (0.12); the launches traced: 596 us -> 75.2 us
  waiting for transfers between devices: 510 us -> 0 us
  Pallas kernels: 0 us -> 69.9 us
  local copies, waits for them, and re-layouts: 41.1 us -> 4.61 us
  matrix products: 26.9 us -> 0 us
  between operations: 13.9 us -> 0.64 us
    psum x1 -> x0, waiting for transfers between devices: 263 us -> none  [local(): weight_grad = lax.psum(grad_term, ('row', 'col')) * scale]
    all_gather x2 -> x0, waiting for transfers between devices: 108 us -> none  [the longest x1 67.5 us: local(): gathered = lax.all_gather(x_feat, 'row', axis=1, tiled=True)]
    reduce_scatter x1 -> x0, waiting for transfers between devices: 75.2 us -> none  [local(): lax.psum_scatter(partial_value.astype(jnp.bfloat16), 'col', scatter_dimen...]
    pallas_call x0 -> x1, Pallas kernels: none -> 69.9 us  [layer_call(): pl.pallas_call(functools.partial(layer_kernel, scale), out_shape=(jax.Sha...]
    unnamed x6 -> x0, waiting for transfers between devices: 63.6 us -> none
    dot_general x7 -> x0, matrix products: 26.9 us -> none  [the longest x2 7.5 us: place_tiles(): placed = jnp.einsum('ts,sif->tif', onehot, prods)]
    dot_general x2 -> x0, local copies, waits for them, and re-layouts: 17.9 us -> none  [the longest x1 8.99 us: slot_products(): jnp.einsum('sji,sjf->sif', vals, picked, preferred_element_type=jnp.float32)]
    gather x2 -> x0, local copies, waits for them, and re-layouts: 14.8 us -> none  [slot_products(): picked = jnp.take(ftiles, index, axis=0)]
  transfers between devices with their start and end apart: 5 -> 0, of which waited for: 5 -> 0; matrix products, arithmetic and copies ran while one was open for 12% -> 0% of each run, Pallas kernels for 0% -> 0%
where the time goes in v2:
time: 75.4 us; the launch traced here: 75.2 us
  Pallas kernels  69.9 us (93%)
  local copies, waits for them, and re-layouts  4.61 us (6%)
    pallas_call x1, Pallas kernels, layer_call(): pl.pallas_call(functools.partial(layer_kernel, scale), out_shape=(jax.Sha...  69.9 us
    unnamed x3, local copies, waits for them, and re-layouts  4.61 us

profile of v2, /device:TPU:1, one launch (start us, length us, event | category | flops | bytes accessed | tf_op | source)
XLA Modules:
  0.0 75.2 jit_solution(13394066162795837963)
XLA Ops:
  0.6 69.9 %graph_layer.1 = (bf16[128,256]{1,0:T(8,128)(2,1)}, bf16[16,2048]{1,0:T(8,128)(2,1)}, f32[256,256]{1,0:T(8,128)}) custom-call(bf16[16,2048]{1,0:T(8,128)(2,1)} %bitcast.4, bf16[16,16,256]{2,1,0:T(8,128)(2,1)} %bitcast.3, bf16[1,1,96,128,128]{4,3,2,1,0:T(8,128)(2,1)} %vals_in.1, s32[1,1,96]{2,1,0:T(1,128)} %trow_in.1, s32[1,1,96]{2,1,0:T(1,128)} %tcol_in.1, ...), custom_call_target="tpu_custom_call" | custom-call | tf_op jit(solution)/shard_map/graph_layer/pallas_call | solution.py:415
  70.6 1.5 %copy.13 = bf16[128,256]{1,0:T(8,128)(2,1)} copy(bf16[128,256]{1,0:T(8,128)(2,1)} %get-tuple-element.12) | data formatting | bytes 131072
  72.0 1.7 %copy.14 = f32[256,256]{1,0:T(8,128)} copy(f32[256,256]{1,0:T(8,128)} %get-tuple-element.13) | data formatting | bytes 524288
  73.7 1.5 %copy.15 = bf16[2048,16]{0,1:T(8,128)(2,1)} copy(bf16[2048,16]{0,1:T(8,128)(2,1)} %bitcast.5) | data formatting | bytes 131072

commit v3 on v2

--- a/solution.py
+++ b/solution.py
@@ -224,7 +224,7 @@
     to_scalars.wait()
     load[6].wait()
 
-    def run(base, source, contract):
+    def run(base, source, contract, begin=0, end=SLOTS // RUN, acc=None):
         def step(i, acc):
             for v in range(RUN):
                 s = i * RUN + v
@@ -234,7 +234,8 @@
                 acc = jnp.where(same, acc + prod, prod)
                 runs[s] = acc.astype(BF)
             return acc
-        lax.fori_loop(0, SLOTS // RUN, step, jnp.zeros((F, TILE), F32))
+        acc = jnp.zeros((F, TILE), F32) if acc is None else acc
+        return lax.fori_loop(begin, end, step, acc)
 
     def last_of(base, t):
         count = meta[base + 3, t]
@@ -296,17 +297,6 @@
                 mid[half[d]] = total_of([own.at[half[d]], b3.at[side[d], u, half[d]], b4.at[side[d], u]])
                 wire.start(b2s[d, u], mid, b2.at[side[d], u], at(dz=2 * d))
 
-    for j in order:
-        wire.landed(cs[j], core_in.at[yy(j)], sib)
-
-        def add(i, carry):
-            c[yy(j), i] = total_of([pt.at[yy(j), i, k], core_in.at[yy(j), i]])
-            return carry
-
-        lax.fori_loop(0, NX, add, 0)
-        for o in near:
-            wire.start(pxs[j, o], c.at[yy(j), (x + o) % NX], xin.at[o - 1, j], at(dx=o))
-
     def spread(i, carry):
         for v in range(UNROLL):
             t = i * UNROLL + v
@@ -314,21 +304,22 @@
             bt[:, :, t] = term.astype(BF).reshape(NZ, NYL, F // N_ROW, TILE)
         return carry
 
-    for j in (0, 3, 1, 2):
-        for dx in range(4):
-            wire.landed(dks[j, dx], piece(j, dx, 1), sib)
-
-    run(4, lambda i: dg[i], (((1,), (0,)), ((), ())))
-    lax.fori_loop(0, TC // UNROLL, spread, 0)
-    b_start()
+    for j in order:
+        wire.landed(cs[j], core_in.at[yy(j)], sib)
+
+        def add(i, carry):
+            c[yy(j), i] = total_of([pt.at[yy(j), i, k], core_in.at[yy(j), i]])
+            return carry
+
+        lax.fori_loop(0, NX, add, 0)
 
     def grad_term(i, total):
-        for v in range(UNROLL):
+        for v in range(NX):
             total += lax.dot_general(
-                pt[i, v // NK, v % NK], dg[i * UNROLL + v], NT, preferred_element_type=F32)
+                c[i, v], dg[(i * NX + v) * NK + k], NT, preferred_element_type=F32)
         return total
 
-    total = lax.fori_loop(0, TR // UNROLL, grad_term, jnp.zeros((F, F), F32)).astype(BF)
+    total = lax.fori_loop(0, NYH, grad_term, jnp.zeros((F, F), F32)).astype(BF)
     for i in range(NZ):
         for u in (0, 1):
             b, a = (i * NYL + u) * 16, at(dz=i - 1, dyl=u)[0]
@@ -352,6 +343,23 @@
 
     g_exchange(0, plane_x, lambda o: g.at[pl.ds((m + o) % 8 * 4, 4)])
 
+    for j in order:
+        for o in near:
+            wire.start(pxs[j, o], c.at[yy(j), (x + o) % NX], xin.at[o - 1, j], at(dx=o))
+
+    for j in (0, 3, 1, 2):
+        for dx in range(4):
+            wire.landed(dks[j, dx], piece(j, dx, 1), sib)
+
+    part = run(4, lambda i: dg[i], (((1,), (0,)), ((), ())), 0, 1)
+    g_add(0, g.at[pl.ds(m * 4, 4)])
+    g_exchange(1, plane_z, lambda o: g_part.at[0])
+    run(4, lambda i: dg[i], (((1,), (0,)), ((), ())), 1, SLOTS // RUN, part)
+    lax.fori_loop(0, TC // UNROLL, spread, 0)
+    b_start()
+    g_add(1, g_part.at[0])
+    g_exchange(2, plane_y, lambda o: g_part.at[1])
+
     def p_x_landed(j):
         for o in near:
             wire.landed(pxs[j, o], xin.at[o - 1, j], at(dx=-o))
@@ -359,22 +367,13 @@
         if j:
             wire.start(pys[j], dsum.at[j], yin.at[j - 1], at(dyh=j))
 
-    p_x_landed(2)
-    b_middle()
-    p_x_landed(1)
-
-    g_add(0, g.at[pl.ds(m * 4, 4)])
-    g_exchange(1, plane_y, lambda o: g_part.at[0])
-
-    p_x_landed(3)
-
-    g_add(1, g_part.at[0])
-    g_exchange(2, plane_z, lambda o: g_part.at[1])
-
-    p_x_landed(0)
-
     g_add(2, g_part.at[1])
     g_exchange(3, plane_x, lambda o: g_part.at[2])
+    p_x_landed(2)
+    p_x_landed(1)
+    b_middle()
+    p_x_landed(3)
+    p_x_landed(0)
 
     for u in (1, 0):
         for d in (1, -1):

time: 75.4 us -> 70.1 us (0.930)
  Pallas kernels: 69.9 us -> 64.6 us
    pallas_call x1, Pallas kernels: 69.9 us -> 64.6 us  [layer_call(): pl.pallas_call(functools.partial(layer_kernel, scale), out_shape=(jax.Sha...]
where the time goes in v3:
time: 70.1 us; the launch traced here: 69.9 us
  Pallas kernels  64.6 us (92%)
  local copies, waits for them, and re-layouts  4.61 us (7%)
    pallas_call x1, Pallas kernels, layer_call(): pl.pallas_call(functools.partial(layer_kernel, scale), out_shape=(jax.Sha...  64.6 us
    unnamed x3, local copies, waits for them, and re-layouts  4.61 us

profile of v3, /device:TPU:1, one launch (start us, length us, event | category | flops | bytes accessed | tf_op | source)
XLA Modules:
  0.0 69.9 jit_solution(16220687355970893456)
XLA Ops:
  0.6 64.6 %graph_layer.1 = (bf16[128,256]{1,0:T(8,128)(2,1)}, bf16[16,2048]{1,0:T(8,128)(2,1)}, f32[256,256]{1,0:T(8,128)}) custom-call(bf16[16,2048]{1,0:T(8,128)(2,1)} %bitcast.4, bf16[16,16,256]{2,1,0:T(8,128)(2,1)} %bitcast.3, bf16[1,1,96,128,128]{4,3,2,1,0:T(8,128)(2,1)} %vals_in.1, s32[1,1,96]{2,1,0:T(1,128)} %trow_in.1, s32[1,1,96]{2,1,0:T(1,128)} %tcol_in.1, ...), custom_call_target="tpu_custom_call" | custom-call | tf_op jit(solution)/shard_map/graph_layer/pallas_call | solution.py:414
  65.3 1.5 %copy.13 = bf16[128,256]{1,0:T(8,128)(2,1)} copy(bf16[128,256]{1,0:T(8,128)(2,1)} %get-tuple-element.12) | data formatting | bytes 131072
  66.8 1.7 %copy.14 = f32[256,256]{1,0:T(8,128)} copy(f32[256,256]{1,0:T(8,128)} %get-tuple-element.13) | data formatting | bytes 524288
  68.4 1.5 %copy.15 = bf16[2048,16]{0,1:T(8,128)(2,1)} copy(bf16[2048,16]{0,1:T(8,128)(2,1)} %bitcast.5) | data formatting | bytes 131072

commit v4 on v3

--- a/solution.py
+++ b/solution.py
@@ -63,7 +63,7 @@
 
 N_LINK = 1 + 16 + 3 + 12 + 16 + 4 + 12 + 3 + 16 + 1
 UNROLL = 8
-RUN = 32
+RUN = 48
 NT = (((1,), (1,)), ((), ()))
 TN = (((0,), (0,)), ((), ()))
 
@@ -91,7 +91,7 @@
     rows[3:4, :] = jnp.sum((key_down <= lane).astype(jnp.int32), axis=0, keepdims=True)
 
 
-def layer_kernel(scale, x_in, w_in, vals_in, trow_in, tcol_in, live_in, d_in, layer, feat, wgrad,
+def layer_kernel(scale, x_in, w_in, vals_in, idx_in, d_in, layer, feat, wgrad,
                  wl, w, vals, idx, keys, meta_v, meta, xl, dl, xg, dg, runs, pt, bt,
                  core_in, c, xin, dsum, yin, b1, b2, b3, b4, bmid, e, ylr, g, g_in, g_part,
                  loads, send, recv, gsend, grecv):
@@ -124,7 +124,7 @@
         pltpu.make_async_copy(src, dst, loads.at[i])
         for i, (src, dst) in enumerate((
             (x_in, xl), (d_in, dl),
-            (trow_in.at[0], idx.at[0]), (tcol_in.at[0], idx.at[1]), (live_in.at[0], idx.at[2]),
+            (idx_in, idx),
             (w_in, wl), (vals_in.at[0, 0], vals)))
     ]
     for copy in load:
@@ -195,11 +195,9 @@
         wire.start(dys[o], piece(0), piece(0), at(dyh=o))
     d_to_x(0)
 
-    for copy in load[2:5]:
-        copy.wait()
+    load[2].wait()
     keys[...] = jnp.full(keys.shape, TILE - 1, jnp.int32)
-    for i in range(3):
-        keys[i:i + 1, 0:SLOTS] = idx[i]
+    keys[0:3, 0:SLOTS] = idx[...]
     alive = keys[2:3, :] > 0
     sorted_rows(jnp.where(alive, keys[0:1, :], TR), keys[1:2, :], meta_v.at[0:4])
     wire.landed(ys, xg.at[1, 1], ylo)
@@ -216,13 +214,13 @@
     wire.landed(dys[2], piece(2), at(dyh=2))
     d_to_x(2)
     d_x_landed(0)
-    load[5].wait()
+    load[3].wait()
     for i in range(NZ):
         for u in (0, 1):
             b = (i * NYL + u) * (F // N_ROW)
             w[b:b + F // N_ROW, :] = wl[at(dz=i - 1, dyl=u)[0]]
     to_scalars.wait()
-    load[6].wait()
+    load[4].wait()
 
     def run(base, source, contract, begin=0, end=SLOTS // RUN, acc=None):
         def step(i, acc):
@@ -406,7 +404,7 @@
     wire.drain()
 
 
-def layer_call(xt, w, vals, trow, tcol, live, d_out, scale):
+def layer_call(xt, w, vals, idx, d_out, scale):
     vmem = pl.BlockSpec(memory_space=pltpu.VMEM)
     here = pl.BlockSpec(memory_space=pltpu.HBM)
     fr = F // N_ROW
@@ -418,13 +416,13 @@
             jax.ShapeDtypeStruct((fr, TC * TILE), BF),
             jax.ShapeDtypeStruct((F, F), F32),
         ),
-        in_specs=[here] * 7,
+        in_specs=[here] * 5,
         out_specs=(vmem, vmem, vmem),
         scratch_shapes=[
             pltpu.VMEM((N_ROW, F // N_ROW, F), BF),
             pltpu.VMEM((F, F), BF),
             pltpu.VMEM((SLOTS, TILE, TILE), BF),
-            pltpu.VMEM((3, 1, SLOTS), ints),
+            pltpu.VMEM((3, SLOTS), ints),
             pltpu.VMEM((8, TILE), ints),
             pltpu.VMEM((8, TILE), ints),
             pltpu.SMEM((8, TILE), ints),
@@ -450,22 +448,23 @@
             pltpu.VMEM((N_COL, 16, TILE), BF),
             pltpu.VMEM((4, 8, 4, 16, TILE), BF),
             pltpu.VMEM((3, 4, 16, TILE), BF),
-            pltpu.SemaphoreType.DMA((7,)),
+            pltpu.SemaphoreType.DMA((5,)),
             pltpu.SemaphoreType.DMA((N_LINK,)),
             pltpu.SemaphoreType.DMA((N_LINK,)),
             pltpu.SemaphoreType.DMA((4,)),
             pltpu.SemaphoreType.DMA((4,)),
         ],
         compiler_params=pltpu.CompilerParams(
-            collective_id=0, has_side_effects=True, vmem_limit_bytes=56 << 20),
+            collective_id=0, has_side_effects=True, vmem_limit_bytes=55040 << 10),
         name="graph_layer",
-    )(xt, w.reshape(N_ROW, fr, F), vals, trow, tcol, live, d_out)
+    )(xt, w.reshape(N_ROW, fr, F), vals, idx, d_out)
 
 
 def local(x_feat, weight, tile_vals, tile_row, tile_col, tile_live, d_out):
     nodes = d_out.shape[0] * N_COL * N_ROW
+    idx = jnp.concatenate([tile_row[0], tile_col[0], tile_live[0]], axis=0)
     layer, feat, wgrad = layer_call(
-        x_feat.T, weight, tile_vals, tile_row, tile_col, tile_live, d_out, 1.0 / math.sqrt(nodes))
+        x_feat.T, weight, tile_vals, idx, d_out, 1.0 / math.sqrt(nodes))
     return layer, wgrad, feat.T
 
 

time: 70.1 us -> 68.8 us (0.981)
  local copies, waits for them, and re-layouts: 4.61 us -> 2.93 us
    unnamed x3, local copies, waits for them, and re-layouts: 4.61 us -> 2.93 us
where the time goes in v4:
time: 68.8 us; the launch traced here: 68.3 us
  Pallas kernels  64 us (93%)
  local copies, waits for them, and re-layouts  2.93 us (4%)
  other arithmetic  0.7 us (1%)
    pallas_call x1, Pallas kernels, layer_call(): pl.pallas_call(functools.partial(layer_kernel, scale), out_shape=(jax.Sha...  64 us
    unnamed x3, local copies, waits for them, and re-layouts  2.93 us

profile of v4, /device:TPU:1, one launch (start us, length us, event | category | flops | bytes accessed | tf_op | source)
XLA Modules:
  0.0 68.3 jit_solution(5722918587766700755)
XLA Ops:
  0.6 0.7 %pad_add_fusion.idx_in = s32[3,96]{1,0:T(4,128)S(1)} fusion(s32[1,96]{1,0:T(1,128)} %bitcast.9, s32[1,96]{1,0:T(1,128)} %bitcast.10, s32[1,96]{1,0:T(1,128)} %bitcast.11), kind=kLoop, calls=%fused_computation | loop fusion | flops 576 | bytes 2304 | tf_op jit(solution)/shard_map/concatenate | solution.py:465
  1.3 64.0 %graph_layer.1 = (bf16[128,256]{1,0:T(8,128)(2,1)S(1)}, bf16[16,2048]{1,0:T(8,128)(2,1)S(1)}, f32[256,256]{1,0:T(8,128)}) custom-call(bf16[16,2048]{1,0:T(8,128)(2,1)} %bitcast.8, bf16[16,16,256]{2,1,0:T(8,128)(2,1)} %bitcast.7, bf16[1,1,96,128,128]{4,3,2,1,0:T(8,128)(2,1)} %vals_in.1, s32[3,96]{1,0:T(4,128)S(1)} %pad_add_fusion.idx_in, bf16[128,256]{1,0:T(8,128)(2,1)} %d_in.1), custom_call_target="tpu_custom_call" | custom-call | tf_op jit(solution)/shard_map/graph_layer/pallas_call | solution.py:412
  65.4 0.6 copy.13
  66.0 1.7 %copy.14 = f32[256,256]{1,0:T(8,128)} copy(f32[256,256]{1,0:T(8,128)} %get-tuple-element.13) | data formatting | bytes 524288
  67.7 0.6 copy.15
